TPU v7x, 1024 devices: a whole 8x8x8 slice. The times are simulated.
1024 devices in a mesh: ctx: 8 (over z_hi, core), tp: 8 (over x), dp: 16 (over y, z_lo).
Axes of the slice: x: 8, y: 8, z: 8 (z_hi: 4, z_lo: 2; z = z_hi * 2 + z_lo), core: 2. Of those that a mesh axis runs over, the one named last changes fastest.
Arguments:
- grad_out: bfloat16 [16, 1024, 4096], P('dp', 'ctx'), may hold values from -6 to 6
- expert_input: bfloat16 [8, 16, 8, 19, 4096], P('ctx', 'dp'), may hold values from -6 to 6
- expert_ids: int32 [16, 1024], P('dp', 'ctx'), may hold values from 0 to 7, as said below
- slots: int32 [16, 1024], P('dp', 'ctx'), may hold values from 0 to 18, as said below
- w_gate: bfloat16 [8, 4096, 2048], P('ctx', None, 'tp'), may hold values from -0.09375 to 0.09375
- w_up: bfloat16 [8, 4096, 2048], P('ctx', None, 'tp'), may hold values from -0.09375 to 0.09375
- w_down: bfloat16 [8, 2048, 4096], P('ctx', 'tp'), may hold values from -0.125 to 0.125
Outputs:
- grad_input: bfloat16 [16, 1024, 4096], P('dp', 'ctx', 'tp')
- grad_gate: float32 [8, 4096, 2048], P('ctx', 'dp', 'tp')
- grad_up: float32 [8, 4096, 2048], P('ctx', 'dp', 'tp')
Inputs may be any that keep to these rules, and one draw needn't show every extreme that they name: `expert_ids`: among the 128 tokens of one source of a group, no expert is named more than 19 times, and in every group one expert is named exactly 19 times by every source. Tokens of one source of a group that name the same expert have different slots.
All inputs are finite; a program needn't handle non-finite values.
Results may differ from a plain program's by a relative error of at most 0.022.
Values may be sent and summed in bfloat16 or wider, within the bound.
A program may use at most 64 MiB of HBM per device.

v0:
```python
import jax
import jax.numpy as jnp
from jax import lax
from jax.sharding import PartitionSpec as P


def body(grad_out, expert_input, expert_ids, slots, w_gate, w_up, w_down):
    ctx_count = lax.axis_size("ctx")
    dp_count = lax.axis_size("dp")
    capacity = expert_input.shape[3]
    model_width = grad_out.shape[2]
    rows_exp = ctx_count * capacity
    block_ff = w_gate.shape[2]
    contract_last = (((1,), (1,)), ((), ()))
    contract_first = (((0,), (0,)), ((), ()))
    tokens = grad_out[0]
    position = expert_ids[0] * capacity + slots[0]
    saved = expert_input.reshape(rows_exp, model_width)
    gate_weights = w_gate[0]
    up_weights = w_up[0]
    down_weights = w_down[0]
    outgoing = jnp.zeros((rows_exp, model_width), jnp.bfloat16).at[position].set(tokens)
    incoming = lax.all_to_all(
        outgoing.reshape(ctx_count, capacity, model_width),
        "ctx",
        split_axis=0,
        concat_axis=0,
        tiled=True,
    )
    grad_hidden = lax.dot_general(
        incoming.reshape(rows_exp, model_width),
        down_weights,
        contract_last,
        preferred_element_type=jnp.float32,
    )
    gate = jnp.dot(saved, gate_weights, preferred_element_type=jnp.float32)
    upward = jnp.dot(saved, up_weights, preferred_element_type=jnp.float32)
    sigmoid_gate = jax.nn.sigmoid(gate)
    grad_gate_pre = (
        grad_hidden * upward * sigmoid_gate * (1.0 + gate * (1.0 - sigmoid_gate))
    ).astype(jnp.bfloat16)
    grad_up_pre = (grad_hidden * gate * sigmoid_gate).astype(jnp.bfloat16)
    partial_value = lax.dot_general(
        grad_gate_pre, gate_weights, contract_last, preferred_element_type=jnp.float32
    )
    partial_value = partial_value + lax.dot_general(
        grad_up_pre, up_weights, contract_last, preferred_element_type=jnp.float32
    )
    outgoing_back = partial_value.astype(jnp.bfloat16).reshape(ctx_count, capacity, model_width)
    returned = lax.all_to_all(
        outgoing_back, "ctx", split_axis=0, concat_axis=0, tiled=True
    ).reshape(rows_exp, model_width)
    token_rows = returned[position].astype(jnp.float32)
    grad_input = lax.psum_scatter(
        token_rows.astype(jnp.bfloat16), "tp", scatter_dimension=1, tiled=True
    )
    hidden_cat = jnp.concatenate([grad_gate_pre, grad_up_pre], axis=1)
    weight_grad = lax.psum_scatter(
        lax.dot_general(
            saved, hidden_cat, contract_first, preferred_element_type=jnp.float32
        ).astype(jnp.bfloat16),
        "dp",
        scatter_dimension=0,
        tiled=True,
    ).astype(jnp.float32)
    weight_grad = weight_grad / dp_count
    return (grad_input[None], weight_grad[:, :block_ff][None], weight_grad[:, block_ff:][None])


def solution(mesh):
    return jax.shard_map(
        body,
        mesh=mesh,
        in_specs=(
            P("dp", "ctx", None),
            P("ctx", "dp", None, None, None),
            P("dp", "ctx"),
            P("dp", "ctx"),
            P("ctx", None, "tp"),
            P("ctx", None, "tp"),
            P("ctx", "tp", None),
        ),
        out_specs=(P("dp", "ctx", "tp"), P("ctx", "dp", "tp"), P("ctx", "dp", "tp")),
        check_vma=False,
    )
```

profile of v0, /device:TPU:1, one launch (start us, length us, event | category | flops | bytes accessed | tf_op | source)
XLA Modules:
  0.0 260.9 jit_solution(6058461041572677350)
XLA Ops:
  7.2 0.8 fusion.29
  8.0 3.1 %scatter_custom_fusion = bf16[152,4096]{1,0:T(8,128)(2,1)S(1)} fusion(s32[128]{0:T(128)S(1)} %fusion.29, bf16[1,128,4096]{2,1,0:T(8,128)(2,1)} %param.7, bf16[]{:T(256)} %constant.1.clone.1), kind=kCustom, calls=%fused_computation.19 | custom fusion | bytes 2293762 | tf_op jit(solution)/shard_map/scatter | solution.py:22
  11.1 1.6 reshape.53
  12.7 18.5 %all-to-all-start = ((bf16[8,19,4096]{2,1,0:T(8,128)(2,1)}), bf16[8,19,4096]{2,1,0:T(8,128)(2,1)}, u32[]{:S(2)}, u32[]{:S(2)}) async-start(bf16[8,19,4096]{2,1,0:T(8,128)(2,1)} %reshape.53), calls=%async_computation | async-start | bytes 3145728 | tf_op jit(solution)/shard_map/all_to_all | solution.py:23
  31.1 1.9 copy.12
  33.0 1.8 reshape.55
  34.9 1.2 fusion.4
  36.0 24.9 %all-to-all-done = bf16[8,19,4096]{2,1,0:T(8,128)(2,1)} async-done(((bf16[8,19,4096]{2,1,0:T(8,128)(2,1)}), bf16[8,19,4096]{2,1,0:T(8,128)(2,1)}, u32[]{:S(2)}, u32[]{:S(2)}) %all-to-all-start) | async-done | bytes 1245216 | tf_op jit(solution)/shard_map/all_to_all | solution.py:23
  61.0 2.9 %reshape.54 = bf16[152,4096]{1,0:T(8,128)(2,1)} reshape(bf16[8,19,4096]{2,1,0:T(8,128)(2,1)} %all-to-all-done) | data formatting | bytes 2490368 | tf_op jit(solution)/shard_map/reshape | solution.py:31
  63.8 2.9 %multiply_convert_fusion = (bf16[152,256]{1,0:T(8,128)(2,1)S(1)}, f32[152,256]{1,0:T(8,128)S(1)}) fusion(f32[152,256]{1,0:T(8,128)} %fusion.4, bf16[152,4096]{1,0:T(8,128)(2,1)} %reshape.54, bf16[1,256,4096]{2,1,0:T(8,128)(2,1)} %param.13), kind=kOutput, calls=%fused_computation.28 | convolution fusion | flops 319000576 | bytes 3731456 | tf_op jit(solution)/shard_map/dot_general | solution.py:30
  67.3 3.3 %fusion = bf16[4096,512]{0,1:T(8,128)(2,1)} fusion(bf16[152,4096]{1,0:T(8,128)(2,1)S(1)} %reshape.55, bf16[152,256]{1,0:T(8,128)(2,1)S(1)} %get-tuple-element.11, bf16[152,256]{1,0:T(8,128)(2,1)S(1)} %fusion.20), kind=kOutput, calls=%fused_computation.3 | convolution fusion | flops 639942656 | bytes 5595136 | tf_op jit(solution)/shard_map/dot_general | solution.py:59
  70.6 0.8 fusion.2
  71.4 0.7 copy-done.2
  72.2 0.9 fusion.1
  73.0 1.6 reshape.56
  74.6 15.2 %all-to-all-start.1 = ((bf16[8,19,4096]{2,1,0:T(8,128)(2,1)}), bf16[8,19,4096]{2,1,0:T(8,128)(2,1)}, u32[]{:S(2)}, u32[]{:S(2)}) async-start(bf16[8,19,4096]{2,1,0:T(8,128)(2,1)} %reshape.56), calls=%async_computation.1 | async-start | bytes 3145728 | tf_op jit(solution)/shard_map/all_to_all | solution.py:50
  89.8 68.1 %all-to-all-done.1 = bf16[8,19,4096]{2,1,0:T(8,128)(2,1)} async-done(((bf16[8,19,4096]{2,1,0:T(8,128)(2,1)}), bf16[8,19,4096]{2,1,0:T(8,128)(2,1)}, u32[]{:S(2)}, u32[]{:S(2)}) %all-to-all-start.1) | async-done | bytes 1245216 | tf_op jit(solution)/shard_map/all_to_all | solution.py:50
  157.9 1.9 reshape.57
  159.8 2.2 gather_fusion
  162.0 49.7 %reduce-scatter.5.cloned.1.call-done = bf16[256,512]{0,1:T(8,128)(2,1)} async-done(((bf16[4096,512]{0,1:T(8,128)(2,1)}), bf16[256,512]{0,1:T(8,128)(2,1)}) %reduce-scatter.5.cloned.1.call-update) | async-done | bytes 262160 | tf_op jit(solution)/shard_map/reduce_scatter | solution.py:58
  211.7 1.0 convert_multiply_fusion
  212.7 0.8 copy.13
  213.6 0.8 copy.14
  214.4 39.6 %reduce-scatter.3.cloned.1.call-done = bf16[128,512]{1,0:T(8,128)(2,1)} async-done(((bf16[128,4096]{1,0:T(8,128)(2,1)}), bf16[128,512]{1,0:T(8,128)(2,1)}) %reduce-scatter.3.cloned.1.call-update) | async-done | bytes 131088 | tf_op jit(solution)/shard_map/reduce_scatter | solution.py:54
  (16 shorter events, 0.6 us)
Async XLA Ops:
  7.2 27.7 %copy-start = (bf16[1,4096,256]{2,1,0:T(8,128)(2,1)S(1)}, bf16[1,4096,256]{2,1,0:T(8,128)(2,1)}, u32[]{:S(2)}) copy-start(bf16[1,4096,256]{2,1,0:T(8,128)(2,1)} %param.11) | copy-start | bytes 6291460
  12.7 18.5 %copy-start.3 = (bf16[1,1,8,19,4096]{4,2,3,1,0:T(8,128)(2,1)S(1)}, bf16[1,1,8,19,4096]{4,2,3,1,0:T(8,128)(2,1)}, u32[]{:S(2)}) copy-start(bf16[1,1,8,19,4096]{4,2,3,1,0:T(8,128)(2,1)} %param.8) | copy-start | bytes 3735556
  12.7 48.3 %all-to-all-start = ((bf16[8,19,4096]{2,1,0:T(8,128)(2,1)}), bf16[8,19,4096]{2,1,0:T(8,128)(2,1)}, u32[]{:S(2)}, u32[]{:S(2)}) async-start(bf16[8,19,4096]{2,1,0:T(8,128)(2,1)} %reshape.53), calls=%async_computation | async-start | bytes 3145728 | tf_op jit(solution)/shard_map/all_to_all | solution.py:23
  31.1 180.6 %reduce-scatter.5.cloned.1.call-start = ((), (), s32[]{:S(2)}) async-start(), calls=%async_computation.5 | async-start | bytes 4456448 | tf_op jit(solution)/shard_map/reduce_scatter | solution.py:58
  63.8 2.9 %copy-start.1 = (bf16[1,4096,256]{2,1,0:T(8,128)(2,1)S(1)}, bf16[1,4096,256]{2,1,0:T(8,128)(2,1)}, u32[]{:S(2)}) copy-start(bf16[1,4096,256]{2,1,0:T(8,128)(2,1)} %param.12) | copy-start | bytes 6291460
  63.8 2.9 %copy-start.4 = (f32[152,256]{1,0:T(8,128)S(1)}, f32[152,256]{1,0:T(8,128)}, u32[]{:S(2)}) copy-start(f32[152,256]{1,0:T(8,128)} %fusion.4) | copy-start | bytes 466948
  70.6 1.6 copy-start.2
  74.6 83.3 %all-to-all-start.1 = ((bf16[8,19,4096]{2,1,0:T(8,128)(2,1)}), bf16[8,19,4096]{2,1,0:T(8,128)(2,1)}, u32[]{:S(2)}, u32[]{:S(2)}) async-start(bf16[8,19,4096]{2,1,0:T(8,128)(2,1)} %reshape.56), calls=%async_computation.1 | async-start | bytes 3145728 | tf_op jit(solution)/shard_map/all_to_all | solution.py:50
  89.8 164.2 %reduce-scatter.3.cloned.1.call-start = ((), (), s32[]{:S(2)}) async-start(), calls=%async_computation.4 | async-start | bytes 1179648 | tf_op jit(solution)/shard_map/reduce_scatter | solution.py:54
Sparse Core Ops, SparseCore 0:
  70.7 140.9 reduce-scatter.4
  215.7 38.2 reduce-scatter.2
where the time goes:
time: 265 us; the launch traced here: 261 us
  waiting for transfers between devices  182 us (69%)
  starting transfers between devices  33.6 us (13%)
  local copies, waits for them, and re-layouts  19.3 us (7%)
  between operations  14.1 us (5%)
  matrix products  9.57 us (4%)
    all_to_all x1, waiting for transfers between devices, body(): lax.all_to_all(outgoing_back, 'ctx', split_axis=0, concat_axis=0, tiled=T...  68.1 us
    reduce_scatter x1, waiting for transfers between devices, body(): lax.psum_scatter(lax.dot_general(saved, hidden_cat, contract_first, prefe...  49.7 us
    reduce_scatter x1, waiting for transfers between devices, body(): lax.psum_scatter(token_rows.astype(jnp.bfloat16), 'tp', scatter_dimension...  39.6 us
    all_to_all x1, waiting for transfers between devices, body(): lax.all_to_all(outgoing.reshape(ctx_count, capacity, model_width), 'ctx',...  24.9 us
    all_to_all x1, starting transfers between devices, body(): lax.all_to_all(outgoing.reshape(ctx_count, capacity, model_width), 'ctx',...  18.5 us
    all_to_all x1, starting transfers between devices, body(): lax.all_to_all(outgoing_back, 'ctx', split_axis=0, concat_axis=0, tiled=T...  15.2 us
  transfers between devices with their start and end apart: 4, of which 4 were waited for; matrix products, arithmetic and copies ran while one was open for 6% of the time, Pallas kernels for 0%

commit v1 on v0

v1 whole, which is shorter than its diff:
```python
import jax
import jax.numpy as jnp
from jax import lax
from jax.experimental import pallas as pl
from jax.experimental.pallas import tpu as pltpu
from jax.sharding import PartitionSpec as P

MESH = pl.DeviceIdType.MESH
BF16 = jnp.bfloat16
F32 = jnp.float32

RING = 8
CAP = 19
ROWS = RING * CAP
MAIN = 16
TOK = 128
D = 4096
FEAT = D // RING
H = FEAT // 2
FB = 256
PACK = FEAT + 128


def mm(a, b, ca, cb):
    return lax.dot_general(a, b, (((ca,), (cb,)), ((), ())), preferred_element_type=F32)


def iota(shape, dim):
    return lax.broadcasted_iota(jnp.int32, shape, dim)


def onehot(mask):
    return jnp.where(mask, 1.0, 0.0).astype(BF16)


def kernel(
    ids, slots, tok_hbm, x_hbm, wg_hbm, wu_hbm, wd_hbm,
    gi_out, gg_out, gu_out,
    tok, x, wg, wu, wd, route_out, route_in, routed, xt, pa, part, from_left, from_right, back_out, back_in, w_out, w_in,
    load_sem, xload_sem,
    route_ss, route_rs, xt_ss, xt_rs, tp_ss, tp_rs, dp_ss, dp_rs, rs_ss, rs_rs, back_ss, back_rs, w_ss, w_rs,
):
    e, t, d = lax.axis_index("ctx"), lax.axis_index("tp"), lax.axis_index("dp")
    y, a = d // 2, d % 2

    def ctx(s):
        return {"ctx": (e + s) % RING}

    def tp(s):
        return {"tp": (t + s + RING) % RING}

    def dpy(s):
        return {"dp": ((y + s + RING) % RING) * 2 + a}

    twin = {"dp": y * 2 + 1 - a}
    started = []

    def send(src, dst, ss, rs, dev):
        copy = pltpu.make_async_remote_copy(
            src_ref=src, dst_ref=dst, send_sem=ss, recv_sem=rs, device_id=dev, device_id_type=MESH
        )
        copy.start()
        started.append(copy)
        return copy

    load_tok = pltpu.make_async_copy(
        tok_hbm.at[0, :, pl.ds(pl.multiple_of(t * FEAT, FEAT), FEAT)], tok, load_sem.at[0]
    )
    load_tok.start()
    load_x = [
        pltpu.make_async_copy(x_hbm.at[:, pl.ds(j * H, H)], x.at[j], xload_sem.at[j]) for j in range(2 * RING)
    ]
    for copy in load_x:
        copy.start()
    load_wg = pltpu.make_async_copy(wg_hbm.at[0], wg, load_sem.at[1])
    load_wu = pltpu.make_async_copy(wu_hbm.at[0], wu, load_sem.at[2])
    load_wd = pltpu.make_async_copy(wd_hbm.at[0], wd, load_sem.at[3])
    load_wg.start()
    load_wu.start()
    load_wd.start()

    barrier = pltpu.get_barrier_semaphore()
    peers = [ctx(s) for s in range(1, RING)] + [tp(1), tp(-1)] + [dpy(s) for s in range(1, RING)] + [twin]
    for peer in peers:
        pl.semaphore_signal(barrier, inc=1, device_id=peer, device_id_type=MESH)

    expert, slot = ids[...], slots[...]
    main_row = jnp.where(slot < MAIN, expert * MAIN + slot, -1)
    fold_row = jnp.where(slot < MAIN, -8, expert * MAIN + 4 * (slot - MAIN))
    rows = iota((TOK, TOK), 0)
    to_main = onehot(rows == main_row)
    to_fold = [onehot(rows == fold_row + q) for q in range(4)]
    cols = iota((TOK, TOK), 1)
    main_map = onehot(cols == (rows % RING) * MAIN + rows // RING)
    erow = iota((3 * RING, TOK), 0)
    ecol = iota((3 * RING, TOK), 1)
    fold_map = [onehot(ecol == (erow % RING) * MAIN + 4 * (erow // RING) + q) for q in range(4)]

    load_tok.wait()
    mine = tok[...]
    route_out[:, :, :FEAT] = mm(to_main, mine, 1, 0).astype(BF16).reshape(RING, MAIN, FEAT)
    folded = mm(to_fold[0], mine[:, :128], 1, 0)
    for q in range(1, 4):
        folded = folded + mm(to_fold[q], mine[:, 128 * q:128 * q + 128], 1, 0)
    route_out[:, :, FEAT:] = folded.astype(BF16).reshape(RING, MAIN, 128)
    route_in[e] = route_out[e]

    pl.semaphore_wait(barrier, len(peers))
    route = [None] + [
        send(route_out.at[(e + s) % RING], route_in.at[e], route_ss.at[s], route_rs.at[s], ctx(s))
        for s in range(1, RING)
    ]

    for copy in load_x:
        copy.wait()
    xts = {}
    for s in (1, 7, 2, 6, 3, 5, 4):
        for h in range(2):
            xts[s, h] = send(
                x.at[((y + s) % RING) * 2 + h], xt.at[s, h], xt_ss.at[s, h], xt_rs.at[s, h], dpy(s)
            )
    for h in range(2):
        xt[0, h] = x[y * 2 + h]

    load_wg.wait()
    load_wu.wait()
    gate = mm(x[0], wg[:H, :], 1, 0)
    upward = mm(x[0], wu[:H, :], 1, 0)
    for j in range(1, 2 * RING):
        gate = gate + mm(x[j], wg[j * H:j * H + H, :], 1, 0)
        upward = upward + mm(x[j], wu[j * H:j * H + H, :], 1, 0)
    sig = 1.0 / (1.0 + jnp.exp(-gate))
    up_factor = gate * sig
    gate_factor = upward * sig * (1.0 + gate * (1.0 - sig))

    for s in range(1, RING):
        route[s].wait_recv()
    main_in = route_in[:, :, :FEAT].reshape(TOK, FEAT)
    fold_in = route_in[:, :, FEAT:].reshape(TOK, 128)
    main_part = mm(main_map, main_in, 1, 0).astype(BF16)
    fold_part = [mm(m, fold_in, 1, 0).astype(BF16) for m in fold_map]
    for h in range(2):
        routed[0, h, :TOK, :] = main_part[:, h * H:h * H + H]
        routed[0, h, TOK:, :128] = fold_part[2 * h]
        routed[0, h, TOK:, 128:] = fold_part[2 * h + 1]

    def ring_send(buf, ss, rs, k, h, peer, sign):
        src, dst = (k - 1, k) if sign > 0 else ((RING + 1 - k) % RING, RING - k)
        way = 0 if sign > 0 else 1
        return send(buf.at[src, h], buf.at[dst, h], ss.at[way, k - 1, h], rs.at[way, k - 1, h], peer(sign))

    def ring_begin(buf, ss, rs, peer):
        flight = {}
        for h in range(2):
            for sign in (1, -1):
                flight[sign, 1, h] = ring_send(buf, ss, rs, 1, h, peer, sign)
        return flight

    def ring_step(flight, buf, ss, rs, peer, k, h):
        for sign in (1, -1):
            flight[sign, k, h].wait_recv()
            if k < 3 or h == (0 if sign > 0 else 1):
                flight[sign, k + 1, h] = ring_send(buf, ss, rs, k + 1, h, peer, sign)

    def ring_end(flight):
        flight[1, 4, 0].wait_recv()
        flight[-1, 4, 1].wait_recv()

    flight = ring_begin(routed, tp_ss, tp_rs, tp)
    load_wd.wait()

    def hidden_term(s, h):
        first = ((t - s + RING) % RING) * FEAT + h * H
        return mm(routed[s, h], wd[:, pl.ds(pl.multiple_of(first, H), H)], 1, 1)

    grad_hidden = hidden_term(0, 0) + hidden_term(0, 1)
    for k in range(1, 4):
        for h in range(2):
            ring_step(flight, routed, tp_ss, tp_rs, tp, k, h)
            grad_hidden = grad_hidden + hidden_term(k, h) + hidden_term(RING - k, h)
    ring_end(flight)
    grad_hidden = grad_hidden + hidden_term(4, 0) + hidden_term(4, 1)

    grad_gate_pre = (grad_hidden * gate_factor).astype(BF16)
    grad_up_pre = (grad_hidden * up_factor).astype(BF16)
    pa[0, 0] = grad_gate_pre
    pa[0, 1] = grad_up_pre
    dp_flight = ring_begin(pa, dp_ss, dp_rs, dpy)

    def partial_term(j, h):
        first = pl.ds(pl.multiple_of(((t + j) % RING) * FEAT + h * H, H), H)
        part[j, h] = (mm(grad_gate_pre, wg[first, :], 1, 1) + mm(grad_up_pre, wu[first, :], 1, 1)).astype(BF16)

    rs_flight = {}

    def sum_send(sign, k, h):
        way = 0 if sign > 0 else 1
        slot_ = k if sign > 0 else RING - k
        dst = (from_left if sign > 0 else from_right).at[k - 1, h]
        rs_flight[sign, k, h] = send(
            part.at[slot_, h], dst, rs_ss.at[way, k - 1, h], rs_rs.at[way, k - 1, h], tp(sign)
        )

    def sum_step(sign, k, h):
        rs_flight[sign, k + 1, h].wait_recv()
        slot_ = k if sign > 0 else RING - k
        arrived = (from_left if sign > 0 else from_right)[k, h]
        part[slot_, h] = (part[slot_, h].astype(F32) + arrived.astype(F32)).astype(BF16)
        sum_send(sign, k, h)

    partial_term(4, 0)
    sum_send(1, 4, 0)
    partial_term(4, 1)
    sum_send(-1, 4, 1)
    partial_term(3, 1)
    sum_send(1, 3, 1)
    partial_term(5, 0)
    sum_send(-1, 3, 0)
    partial_term(3, 0)
    partial_term(5, 1)

    ring_step(dp_flight, pa, dp_ss, dp_rs, dpy, 1, 0)
    sum_step(1, 3, 0)
    sum_step(-1, 3, 1)
    for j in (2, 6):
        for h in range(2):
            partial_term(j, h)
    ring_step(dp_flight, pa, dp_ss, dp_rs, dpy, 1, 1)
    sum_step(1, 2, 1)
    sum_step(-1, 2, 0)
    ring_step(dp_flight, pa, dp_ss, dp_rs, dpy, 2, 0)
    sum_step(1, 2, 0)
    sum_step(-1, 2, 1)
    for j in (1, 7, 0):
        for h in range(2):
            partial_term(j, h)
    ring_step(dp_flight, pa, dp_ss, dp_rs, dpy, 2, 1)
    sum_step(1, 1, 1)
    sum_step(-1, 1, 0)
    ring_step(dp_flight, pa, dp_ss, dp_rs, dpy, 3, 0)
    sum_step(1, 1, 0)
    sum_step(-1, 1, 1)
    ring_step(dp_flight, pa, dp_ss, dp_rs, dpy, 3, 1)

    for copy in xts.values():
        copy.wait_recv()
    ring_end(dp_flight)

    def weight_term(half, which):
        total = mm(xt[0, half], pa[0, which], 0, 0)
        for s in range(1, RING):
            total = total + mm(xt[s, half], pa[s, which], 0, 0)
        return total

    w_flight = []
    for which in range(2):
        w_out[which] = weight_term(1 - a, which).astype(BF16)
        w_flight.append(send(w_out.at[which], w_in.at[which], w_ss.at[which], w_rs.at[which], twin))

    for h in (1, 0):
        rs_flight[1, 1, h].wait_recv()
        rs_flight[-1, 1, h].wait_recv()
    slot_grad = [
        (part[0, h].astype(F32) + from_left[0, h].astype(F32) + from_right[0, h].astype(F32)).astype(BF16)
        for h in range(2)
    ]
    for h in range(2):
        back_out[:, :, h * H:h * H + H] = mm(main_map, slot_grad[h][:TOK, :], 0, 0).astype(BF16).reshape(RING, MAIN, H)
    folded = mm(fold_map[0], slot_grad[0][TOK:, :128], 0, 0)
    for q in range(1, 4):
        folded = folded + mm(fold_map[q], slot_grad[q // 2][TOK:, (q % 2) * 128:(q % 2) * 128 + 128], 0, 0)
    back_out[:, :, FEAT:] = folded.astype(BF16).reshape(RING, MAIN, 128)
    back_in[e] = back_out[e]
    back = [
        send(back_out.at[(e + s) % RING], back_in.at[e], back_ss.at[s], back_rs.at[s], ctx(s)) for s in range(1, RING)
    ]

    own = [weight_term(a, which) for which in range(2)]

    for copy in back:
        copy.wait_recv()
    main_in = back_in[:, :, :FEAT].reshape(TOK, FEAT)
    fold_in = back_in[:, :, FEAT:].reshape(TOK, 128)
    token_rows = mm(to_main, main_in, 0, 0)
    for q in range(4):
        piece = slice(128 * q, 128 * q + 128)
        gi_out[0, :, piece] = (token_rows[:, piece] + mm(to_fold[q], fold_in, 0, 0)).astype(BF16)

    for which, out in enumerate((gg_out, gu_out)):
        w_flight[which].wait_recv()
        out[0] = (own[which] + w_in[which].astype(F32)) * (1.0 / 16.0)

    for copy in started:
        copy.wait_send()


def body(grad_out, expert_input, expert_ids, slots, w_gate, w_up, w_down):
    saved = expert_input.transpose(0, 1, 3, 2, 4).reshape(ROWS, D)
    vmem = pl.BlockSpec(memory_space=pltpu.VMEM)
    hbm = pl.BlockSpec(memory_space=pl.ANY)
    dma = pltpu.SemaphoreType.DMA
    piece = (2, ROWS, H)
    return pl.pallas_call(
        kernel,
        out_shape=(
            jax.ShapeDtypeStruct((1, TOK, FEAT), BF16),
            jax.ShapeDtypeStruct((1, 256, FB), F32),
            jax.ShapeDtypeStruct((1, 256, FB), F32),
        ),
        in_specs=[vmem, vmem] + [hbm] * 5,
        out_specs=(vmem, vmem, vmem),
        scratch_shapes=[
            pltpu.VMEM((TOK, FEAT), BF16),
            pltpu.VMEM((2 * RING, ROWS, H), BF16),
            pltpu.VMEM((D, FB), BF16),
            pltpu.VMEM((D, FB), BF16),
            pltpu.VMEM((FB, D), BF16),
            pltpu.VMEM((RING, MAIN, PACK), BF16),
            pltpu.VMEM((RING, MAIN, PACK), BF16),
            pltpu.VMEM((RING,) + piece, BF16),
            pltpu.VMEM((RING,) + piece, BF16),
            pltpu.VMEM((RING,) + piece, BF16),
            pltpu.VMEM((RING,) + piece, BF16),
            pltpu.VMEM((4,) + piece, BF16),
            pltpu.VMEM((4,) + piece, BF16),
            pltpu.VMEM((RING, MAIN, PACK), BF16),
            pltpu.VMEM((RING, MAIN, PACK), BF16),
            pltpu.VMEM((2, 256, FB), BF16),
            pltpu.VMEM((2, 256, FB), BF16),
            dma((4,)),
            dma((2 * RING,)),
            dma((RING,)),
            dma((RING,)),
            dma((RING, 2)),
            dma((RING, 2)),
            dma((2, 4, 2)),
            dma((2, 4, 2)),
            dma((2, 4, 2)),
            dma((2, 4, 2)),
            dma((2, 4, 2)),
            dma((2, 4, 2)),
            dma((RING,)),
            dma((RING,)),
            dma((2,)),
            dma((2,)),
        ],
        compiler_params=pltpu.CompilerParams(
            collective_id=0, has_side_effects=True, vmem_limit_bytes=40 * 1024 * 1024
        ),
        name="expert_backward",
    )(expert_ids, slots, grad_out, saved, w_gate, w_up, w_down)


def solution(mesh):
    return jax.shard_map(
        body,
        mesh=mesh,
        in_specs=(
            P("dp", "ctx", None),
            P("ctx", "dp", None, None, None),
            P("dp", "ctx"),
            P("dp", "ctx"),
            P("ctx", None, "tp"),
            P("ctx", None, "tp"),
            P("ctx", "tp", None),
        ),
        out_specs=(P("dp", "ctx", "tp"), P("ctx", "dp", "tp"), P("ctx", "dp", "tp")),
        check_vma=False,
    )
```

time: 265 us -> 89.1 us (0.34); the launches traced: 261 us -> 88.7 us
  waiting for transfers between devices: 182 us -> 0 us
  Pallas kernels: 0 us -> 77.4 us
  starting transfers between devices: 33.6 us -> 0 us
  between operations: 14.1 us -> 0.66 us
  matrix products: 9.57 us -> 0 us
  local copies, waits for them, and re-layouts: 19.3 us -> 10.7 us
    all_to_all x2 -> x0, waiting for transfers between devices: 93.1 us -> none  [the longest x1 68.1 us: body(): lax.all_to_all(outgoing_back, 'ctx', split_axis=0, concat_axis=0, tiled=T...]
    reduce_scatter x2 -> x0, waiting for transfers between devices: 89.3 us -> none  [the longest x1 49.7 us: body(): lax.psum_scatter(lax.dot_general(saved, hidden_cat, contract_first, prefe...]
    pallas_call x0 -> x1, Pallas kernels: none -> 77.4 us  [body(): pl.pallas_call(kernel, out_shape=(jax.ShapeDtypeStruct((1, TOK, FEAT), BF...]
    all_to_all x2 -> x0, starting transfers between devices: 33.6 us -> none  [the longest x1 18.5 us: body(): lax.all_to_all(outgoing.reshape(ctx_count, capacity, model_width), 'ctx',...]
    reshape x5 -> x0, local copies, waits for them, and re-layouts: 9.75 us -> none  [the longest x1 2.88 us: body(): incoming.reshape(rows_exp, model_width)]
    dot_general x6 -> x0, matrix products: 9.57 us -> none  [the longest x1 3.25 us: body(): lax.dot_general(saved, hidden_cat, contract_first, preferred_element_type...]
    unnamed x13 -> x17, local copies, waits for them, and re-layouts: 4.33 us -> 10.7 us
    scatter x1 -> x0, local copies, waits for them, and re-layouts: 3.07 us -> none  [body(): jnp.zeros((rows_exp, model_width), jnp.bfloat16).at[position].set(tokens)]
  transfers between devices with their start and end apart: 4 -> 0, of which waited for: 4 -> 0; matrix products, arithmetic and copies ran while one was open for 6% -> 0% of each run, Pallas kernels for 0% -> 0%
where the time goes in v1:
time: 89.1 us; the launch traced here: 88.7 us
  Pallas kernels  77.4 us (87%)
  local copies, waits for them, and re-layouts  10.7 us (12%)
    pallas_call x1, Pallas kernels, body(): pl.pallas_call(kernel, out_shape=(jax.ShapeDtypeStruct((1, TOK, FEAT), BF...  77.4 us
    unnamed x17, local copies, waits for them, and re-layouts  10.7 us

profile of v1, /device:TPU:1, one launch (start us, length us, event | category | flops | bytes accessed | tf_op | source)
XLA Modules:
  0.0 88.7 jit_solution(9370808518560900163)
XLA Ops:
  0.6 0.0 copy-start
  0.6 1.6 %copy-done = bf16[1,4096,256]{2,1,0:T(8,128)(2,1)S(1)} copy-done((bf16[1,4096,256]{2,1,0:T(8,128)(2,1)S(1)}, bf16[1,4096,256]{2,1,0:T(8,128)(2,1)}, u32[]{:S(2)}) %copy-start) | copy-done | bytes 2097176
  2.2 0.0 copy-start.1
  2.2 1.6 %copy-done.1 = bf16[1,4096,256]{2,1,0:T(8,128)(2,1)S(1)} copy-done((bf16[1,4096,256]{2,1,0:T(8,128)(2,1)S(1)}, bf16[1,4096,256]{2,1,0:T(8,128)(2,1)}, u32[]{:S(2)}) %copy-start.1) | copy-done | bytes 2097176
  3.8 0.0 copy-start.2
  3.8 1.6 %copy-done.2 = bf16[1,256,4096]{2,1,0:T(8,128)(2,1)S(1)} copy-done((bf16[1,256,4096]{2,1,0:T(8,128)(2,1)S(1)}, bf16[1,256,4096]{2,1,0:T(8,128)(2,1)}, u32[]{:S(2)}) %copy-start.2) | copy-done | bytes 2097176
  5.4 0.0 copy-start.3
  5.4 1.3 %copy-done.3 = bf16[1,1,8,19,4096]{4,2,3,1,0:T(8,128)(2,1)S(1)} copy-done((bf16[1,1,8,19,4096]{4,2,3,1,0:T(8,128)(2,1)S(1)}, bf16[1,1,8,19,4096]{4,2,3,1,0:T(8,128)(2,1)}, u32[]{:S(2)}) %copy-start.3) | copy-done | bytes 1245208
  6.7 0.0 copy-start.4
  6.7 1.2 %copy-done.4 = bf16[1,128,4096]{2,1,0:T(8,128)(2,1)S(1)} copy-done((bf16[1,128,4096]{2,1,0:T(8,128)(2,1)S(1)}, bf16[1,128,4096]{2,1,0:T(8,128)(2,1)}, u32[]{:S(2)}) %copy-start.4) | copy-done | bytes 1048600
  7.9 0.0 copy-start.5
  7.9 0.7 copy-done.5
  8.6 0.0 copy-start.6
  8.6 0.7 copy-done.6
  9.2 77.4 %expert_backward.1 = (bf16[1,128,512]{2,1,0:T(8,128)(2,1)S(1)}, f32[1,256,256]{2,1,0:T(8,128)S(1)}, f32[1,256,256]{2,1,0:T(8,128)S(1)}) custom-call(s32[1,128]{1,0:T(1,128)S(1)} %copy-done.5, s32[1,128]{1,0:T(1,128)S(1)} %copy-done.6, bf16[1,128,4096]{2,1,0:T(8,128)(2,1)S(1)} %copy-done.4, bf16[152,4096]{1,0:T(8,128)(2,1)S(1)} %bitcast.3, ...), custom_call_target="tpu_custom_call" | custom-call | tf_op jit(solution)/shard_map/expert_backward/pallas_call | solution.py:303
  86.7 0.7 copy.13
  87.3 0.7 copy.14
  88.0 0.7 copy.15
Async XLA Ops:
  0.6 1.6 %copy-start = (bf16[1,4096,256]{2,1,0:T(8,128)(2,1)S(1)}, bf16[1,4096,256]{2,1,0:T(8,128)(2,1)}, u32[]{:S(2)}) copy-start(bf16[1,4096,256]{2,1,0:T(8,128)(2,1)} %wg_hbm.1) | copy-start | bytes 6291460
  2.2 1.6 %copy-start.1 = (bf16[1,4096,256]{2,1,0:T(8,128)(2,1)S(1)}, bf16[1,4096,256]{2,1,0:T(8,128)(2,1)}, u32[]{:S(2)}) copy-start(bf16[1,4096,256]{2,1,0:T(8,128)(2,1)} %wu_hbm.1) | copy-start | bytes 6291460
  3.8 1.6 %copy-start.2 = (bf16[1,256,4096]{2,1,0:T(8,128)(2,1)S(1)}, bf16[1,256,4096]{2,1,0:T(8,128)(2,1)}, u32[]{:S(2)}) copy-start(bf16[1,256,4096]{2,1,0:T(8,128)(2,1)} %wd_hbm.1) | copy-start | bytes 6291460
  5.4 1.3 %copy-start.3 = (bf16[1,1,8,19,4096]{4,2,3,1,0:T(8,128)(2,1)S(1)}, bf16[1,1,8,19,4096]{4,2,3,1,0:T(8,128)(2,1)}, u32[]{:S(2)}) copy-start(bf16[1,1,8,19,4096]{4,2,3,1,0:T(8,128)(2,1)} %param.8) | copy-start | bytes 3735556
  6.7 1.2 %copy-start.4 = (bf16[1,128,4096]{2,1,0:T(8,128)(2,1)S(1)}, bf16[1,128,4096]{2,1,0:T(8,128)(2,1)}, u32[]{:S(2)}) copy-start(bf16[1,128,4096]{2,1,0:T(8,128)(2,1)} %tok_hbm.1) | copy-start | bytes 3145732
  7.9 0.7 copy-start.5
  8.6 0.7 copy-start.6

commit v2 on v1

--- a/solution.py
+++ b/solution.py
@@ -34,10 +34,10 @@
 
 
 def kernel(
-    ids, slots, tok_hbm, x_hbm, wg_hbm, wu_hbm, wd_hbm,
+    ids_hbm, slots_hbm, tok_hbm, x_hbm, wg_hbm, wu_hbm, wd_hbm,
     gi_out, gg_out, gu_out,
-    tok, x, wg, wu, wd, route_out, route_in, routed, xt, pa, part, from_left, from_right, back_out, back_in, w_out, w_in,
-    load_sem, xload_sem,
+    ids, slots, tok, x, wg, wu, wd, route_out, route_in, routed, xt, pa, part, from_left, from_right, back_out, back_in, w_out, w_in, acc,
+    load_sem, tok_sem, xload_sem,
     route_ss, route_rs, xt_ss, xt_rs, tp_ss, tp_rs, dp_ss, dp_rs, rs_ss, rs_rs, back_ss, back_rs, w_ss, w_rs,
 ):
     e, t, d = lax.axis_index("ctx"), lax.axis_index("tp"), lax.axis_index("dp")
@@ -63,10 +63,19 @@
         started.append(copy)
         return copy
 
-    load_tok = pltpu.make_async_copy(
-        tok_hbm.at[0, :, pl.ds(pl.multiple_of(t * FEAT, FEAT), FEAT)], tok, load_sem.at[0]
-    )
-    load_tok.start()
+    load_ids = pltpu.make_async_copy(ids_hbm, ids, load_sem.at[4])
+    load_slots = pltpu.make_async_copy(slots_hbm, slots, load_sem.at[5])
+    load_ids.start()
+    load_slots.start()
+    load_tok = []
+    for r, c, first in ((0, 0, t * 2), (0, 1, t * 2 + 1), (1, 0, (t + 4) % RING * 2), (1, 1, (t + 4) % RING * 2 + 1),
+                        (2, 0, (t + 5) % RING * 2 + 1), (2, 1, (t + 3) % RING * 2)):
+        load_tok.append(
+            pltpu.make_async_copy(
+                tok_hbm.at[0, :, pl.ds(pl.multiple_of(first * H, H), H)], tok.at[r, c], tok_sem.at[r, c]
+            )
+        )
+        load_tok[-1].start()
     load_x = [
         pltpu.make_async_copy(x_hbm.at[:, pl.ds(j * H, H)], x.at[j], xload_sem.at[j]) for j in range(2 * RING)
     ]
@@ -84,6 +93,8 @@
     for peer in peers:
         pl.semaphore_signal(barrier, inc=1, device_id=peer, device_id_type=MESH)
 
+    load_ids.wait()
+    load_slots.wait()
     expert, slot = ids[...], slots[...]
     main_row = jnp.where(slot < MAIN, expert * MAIN + slot, -1)
     fold_row = jnp.where(slot < MAIN, -8, expert * MAIN + 4 * (slot - MAIN))
@@ -96,20 +107,41 @@
     ecol = iota((3 * RING, TOK), 1)
     fold_map = [onehot(ecol == (erow % RING) * MAIN + 4 * (erow // RING) + q) for q in range(4)]
 
-    load_tok.wait()
-    mine = tok[...]
-    route_out[:, :, :FEAT] = mm(to_main, mine, 1, 0).astype(BF16).reshape(RING, MAIN, FEAT)
-    folded = mm(to_fold[0], mine[:, :128], 1, 0)
-    for q in range(1, 4):
-        folded = folded + mm(to_fold[q], mine[:, 128 * q:128 * q + 128], 1, 0)
-    route_out[:, :, FEAT:] = folded.astype(BF16).reshape(RING, MAIN, 128)
-    route_in[e] = route_out[e]
-
+    def pack(r):
+        load_tok[2 * r].wait()
+        load_tok[2 * r + 1].wait()
+        halves = [tok[r, c] for c in range(2)]
+        for c in range(2):
+            route_out[r, :, :, c * H:c * H + H] = mm(to_main, halves[c], 1, 0).astype(BF16).reshape(RING, MAIN, H)
+        folded = mm(to_fold[0], halves[0][:, :128], 1, 0)
+        for q in range(1, 4):
+            folded = folded + mm(to_fold[q], halves[q // 2][:, (q % 2) * 128:(q % 2) * 128 + 128], 1, 0)
+        route_out[r, :, :, FEAT:] = folded.astype(BF16).reshape(RING, MAIN, 128)
+        route_in[r, e] = route_out[r, e]
+
+    def route_set(r):
+        return [
+            send(
+                route_out.at[r, (e + s) % RING], route_in.at[r, e], route_ss.at[r, s], route_rs.at[r, s], ctx(s)
+            )
+            for s in range(1, RING)
+        ]
+
+    def unpack(r, places):
+        for copy in route[r]:
+            copy.wait_recv()
+        main_in = route_in[r, :, :, :FEAT].reshape(TOK, FEAT)
+        fold_in = route_in[r, :, :, FEAT:].reshape(TOK, 128)
+        main_part = mm(main_map, main_in, 1, 0).astype(BF16)
+        fold_part = [mm(m, fold_in, 1, 0).astype(BF16) for m in fold_map]
+        for c, (s, h) in enumerate(places):
+            routed[s, h, :TOK, :] = main_part[:, c * H:c * H + H]
+            routed[s, h, TOK:, :128] = fold_part[2 * c]
+            routed[s, h, TOK:, 128:] = fold_part[2 * c + 1]
+
+    pack(0)
     pl.semaphore_wait(barrier, len(peers))
-    route = [None] + [
-        send(route_out.at[(e + s) % RING], route_in.at[e], route_ss.at[s], route_rs.at[s], ctx(s))
-        for s in range(1, RING)
-    ]
+    route = [route_set(0)]
 
     for copy in load_x:
         copy.wait()
@@ -122,6 +154,36 @@
     for h in range(2):
         xt[0, h] = x[y * 2 + h]
 
+    for r in (1, 2):
+        pack(r)
+        route.append(route_set(r))
+
+    unpack(0, ((0, 0), (0, 1)))
+
+    def ring_send(buf, ss, rs, k, h, peer, sign):
+        src, dst = (k - 1, k) if sign > 0 else ((RING + 1 - k) % RING, RING - k)
+        way = 0 if sign > 0 else 1
+        return send(buf.at[src, h], buf.at[dst, h], ss.at[way, k - 1, h], rs.at[way, k - 1, h], peer(sign))
+
+    def ring_begin(buf, ss, rs, peer):
+        flight = {}
+        for h in range(2):
+            for sign in (1, -1):
+                flight[sign, 1, h] = ring_send(buf, ss, rs, 1, h, peer, sign)
+        return flight
+
+    def ring_step(flight, buf, ss, rs, peer, k, h, last):
+        for sign in (1, -1):
+            flight[sign, k, h].wait_recv()
+            if k < last - 1 or h == (0 if sign > 0 else 1):
+                flight[sign, k + 1, h] = ring_send(buf, ss, rs, k + 1, h, peer, sign)
+
+    def ring_end(flight, last):
+        flight[1, last, 0].wait_recv()
+        flight[-1, last, 1].wait_recv()
+
+    flight = ring_begin(routed, tp_ss, tp_rs, tp)
+
     load_wg.wait()
     load_wu.wait()
     gate = mm(x[0], wg[:H, :], 1, 0)
@@ -133,40 +195,6 @@
     up_factor = gate * sig
     gate_factor = upward * sig * (1.0 + gate * (1.0 - sig))
 
-    for s in range(1, RING):
-        route[s].wait_recv()
-    main_in = route_in[:, :, :FEAT].reshape(TOK, FEAT)
-    fold_in = route_in[:, :, FEAT:].reshape(TOK, 128)
-    main_part = mm(main_map, main_in, 1, 0).astype(BF16)
-    fold_part = [mm(m, fold_in, 1, 0).astype(BF16) for m in fold_map]
-    for h in range(2):
-        routed[0, h, :TOK, :] = main_part[:, h * H:h * H + H]
-        routed[0, h, TOK:, :128] = fold_part[2 * h]
-        routed[0, h, TOK:, 128:] = fold_part[2 * h + 1]
-
-    def ring_send(buf, ss, rs, k, h, peer, sign):
-        src, dst = (k - 1, k) if sign > 0 else ((RING + 1 - k) % RING, RING - k)
-        way = 0 if sign > 0 else 1
-        return send(buf.at[src, h], buf.at[dst, h], ss.at[way, k - 1, h], rs.at[way, k - 1, h], peer(sign))
-
-    def ring_begin(buf, ss, rs, peer):
-        flight = {}
-        for h in range(2):
-            for sign in (1, -1):
-                flight[sign, 1, h] = ring_send(buf, ss, rs, 1, h, peer, sign)
-        return flight
-
-    def ring_step(flight, buf, ss, rs, peer, k, h):
-        for sign in (1, -1):
-            flight[sign, k, h].wait_recv()
-            if k < 3 or h == (0 if sign > 0 else 1):
-                flight[sign, k + 1, h] = ring_send(buf, ss, rs, k + 1, h, peer, sign)
-
-    def ring_end(flight):
-        flight[1, 4, 0].wait_recv()
-        flight[-1, 4, 1].wait_recv()
-
-    flight = ring_begin(routed, tp_ss, tp_rs, tp)
     load_wd.wait()
 
     def hidden_term(s, h):
@@ -174,12 +202,16 @@
         return mm(routed[s, h], wd[:, pl.ds(pl.multiple_of(first, H), H)], 1, 1)
 
     grad_hidden = hidden_term(0, 0) + hidden_term(0, 1)
-    for k in range(1, 4):
+    for k in range(1, 3):
         for h in range(2):
-            ring_step(flight, routed, tp_ss, tp_rs, tp, k, h)
+            ring_step(flight, routed, tp_ss, tp_rs, tp, k, h, 3)
             grad_hidden = grad_hidden + hidden_term(k, h) + hidden_term(RING - k, h)
-    ring_end(flight)
-    grad_hidden = grad_hidden + hidden_term(4, 0) + hidden_term(4, 1)
+    unpack(1, ((4, 0), (4, 1)))
+    unpack(2, ((3, 1), (5, 0)))
+    for s, h in ((4, 0), (4, 1), (3, 1), (5, 0)):
+        grad_hidden = grad_hidden + hidden_term(s, h)
+    ring_end(flight, 3)
+    grad_hidden = grad_hidden + hidden_term(3, 0) + hidden_term(5, 1)
 
     grad_gate_pre = (grad_hidden * gate_factor).astype(BF16)
     grad_up_pre = (grad_hidden * up_factor).astype(BF16)
@@ -219,42 +251,53 @@
     partial_term(3, 0)
     partial_term(5, 1)
 
-    ring_step(dp_flight, pa, dp_ss, dp_rs, dpy, 1, 0)
+    def dp_step(k, h):
+        ring_step(dp_flight, pa, dp_ss, dp_rs, dpy, k, h, 4)
+
+    def weight_term(s):
+        if s:
+            for h in range(2):
+                xts[s, h].wait_recv()
+        for half in range(2):
+            for which in range(2):
+                term = mm(xt[s, half], pa[s, which], 0, 0)
+                acc[half, which] = acc[half, which] + term if s else term
+
+    dp_step(1, 0)
     sum_step(1, 3, 0)
     sum_step(-1, 3, 1)
     for j in (2, 6):
         for h in range(2):
             partial_term(j, h)
-    ring_step(dp_flight, pa, dp_ss, dp_rs, dpy, 1, 1)
+    dp_step(1, 1)
     sum_step(1, 2, 1)
     sum_step(-1, 2, 0)
-    ring_step(dp_flight, pa, dp_ss, dp_rs, dpy, 2, 0)
+    weight_term(0)
+    dp_step(2, 0)
     sum_step(1, 2, 0)
     sum_step(-1, 2, 1)
     for j in (1, 7, 0):
         for h in range(2):
             partial_term(j, h)
-    ring_step(dp_flight, pa, dp_ss, dp_rs, dpy, 2, 1)
+    dp_step(2, 1)
     sum_step(1, 1, 1)
     sum_step(-1, 1, 0)
-    ring_step(dp_flight, pa, dp_ss, dp_rs, dpy, 3, 0)
+    weight_term(1)
+    weight_term(7)
+    dp_step(3, 0)
     sum_step(1, 1, 0)
     sum_step(-1, 1, 1)
-    ring_step(dp_flight, pa, dp_ss, dp_rs, dpy, 3, 1)
-
-    for copy in xts.values():
-        copy.wait_recv()
-    ring_end(dp_flight)
-
-    def weight_term(half, which):
-        total = mm(xt[0, half], pa[0, which], 0, 0)
-        for s in range(1, RING):
-            total = total + mm(xt[s, half], pa[s, which], 0, 0)
-        return total
-
+    weight_term(2)
+    weight_term(6)
+    dp_step(3, 1)
+    weight_term(3)
+    weight_term(5)
+    for h in range(2):
+        xts[4, h].wait_recv()
+    ring_end(dp_flight, 4)
     w_flight = []
     for which in range(2):
-        w_out[which] = weight_term(1 - a, which).astype(BF16)
+        w_out[which] = (acc[1 - a, which] + mm(xt[4, 1 - a], pa[4, which], 0, 0)).astype(BF16)
         w_flight.append(send(w_out.at[which], w_in.at[which], w_ss.at[which], w_rs.at[which], twin))
 
     for h in (1, 0):
@@ -275,7 +318,7 @@
         send(back_out.at[(e + s) % RING], back_in.at[e], back_ss.at[s], back_rs.at[s], ctx(s)) for s in range(1, RING)
     ]
 
-    own = [weight_term(a, which) for which in range(2)]
+    own = [acc[a, which] + mm(xt[4, a], pa[4, which], 0, 0) for which in range(2)]
 
     for copy in back:
         copy.wait_recv()
@@ -294,29 +337,43 @@
         copy.wait_send()
 
 
+def flush(gi, gg, gu, gi_out, gg_out, gu_out, sems):
+    copies = [
+        pltpu.make_async_copy(src, dst, sems.at[n])
+        for n, (src, dst) in enumerate(((gi, gi_out), (gg, gg_out), (gu, gu_out)))
+    ]
+    for copy in copies:
+        copy.start()
+    for copy in copies:
+        copy.wait()
+
+
 def body(grad_out, expert_input, expert_ids, slots, w_gate, w_up, w_down):
     saved = expert_input.transpose(0, 1, 3, 2, 4).reshape(ROWS, D)
     vmem = pl.BlockSpec(memory_space=pltpu.VMEM)
     hbm = pl.BlockSpec(memory_space=pl.ANY)
     dma = pltpu.SemaphoreType.DMA
     piece = (2, ROWS, H)
-    return pl.pallas_call(
+    shapes = (((1, TOK, FEAT), BF16), ((1, 256, FB), F32), ((1, 256, FB), F32))
+    operands = [
+        pltpu.with_memory_space_constraint(operand, pltpu.HBM)
+        for operand in (expert_ids, slots, grad_out, saved, w_gate, w_up, w_down)
+    ]
+    results = pl.pallas_call(
         kernel,
-        out_shape=(
-            jax.ShapeDtypeStruct((1, TOK, FEAT), BF16),
-            jax.ShapeDtypeStruct((1, 256, FB), F32),
-            jax.ShapeDtypeStruct((1, 256, FB), F32),
-        ),
-        in_specs=[vmem, vmem] + [hbm] * 5,
+        out_shape=tuple(pltpu.VMEM(shape, dtype) for shape, dtype in shapes),
+        in_specs=[hbm] * 7,
         out_specs=(vmem, vmem, vmem),
         scratch_shapes=[
-            pltpu.VMEM((TOK, FEAT), BF16),
+            pltpu.VMEM((1, TOK), jnp.int32),
+            pltpu.VMEM((1, TOK), jnp.int32),
+            pltpu.VMEM((3, 2, TOK, H), BF16),
             pltpu.VMEM((2 * RING, ROWS, H), BF16),
             pltpu.VMEM((D, FB), BF16),
             pltpu.VMEM((D, FB), BF16),
             pltpu.VMEM((FB, D), BF16),
-            pltpu.VMEM((RING, MAIN, PACK), BF16),
-            pltpu.VMEM((RING, MAIN, PACK), BF16),
+            pltpu.VMEM((3, RING, MAIN, PACK), BF16),
+            pltpu.VMEM((3, RING, MAIN, PACK), BF16),
             pltpu.VMEM((RING,) + piece, BF16),
             pltpu.VMEM((RING,) + piece, BF16),
             pltpu.VMEM((RING,) + piece, BF16),
@@ -327,10 +384,12 @@
             pltpu.VMEM((RING, MAIN, PACK), BF16),
             pltpu.VMEM((2, 256, FB), BF16),
             pltpu.VMEM((2, 256, FB), BF16),
-            dma((4,)),
+            pltpu.VMEM((2, 2, 256, FB), F32),
+            dma((6,)),
+            dma((3, 2)),
             dma((2 * RING,)),
-            dma((RING,)),
-            dma((RING,)),
+            dma((3, RING)),
+            dma((3, RING)),
             dma((RING, 2)),
             dma((RING, 2)),
             dma((2, 4, 2)),
@@ -348,7 +407,15 @@
             collective_id=0, has_side_effects=True, vmem_limit_bytes=40 * 1024 * 1024
         ),
         name="expert_backward",
-    )(expert_ids, slots, grad_out, saved, w_gate, w_up, w_down)
+    )(*operands)
+    return pl.pallas_call(
+        flush,
+        out_shape=tuple(jax.ShapeDtypeStruct(shape, dtype) for shape, dtype in shapes),
+        in_specs=[hbm] * 3,
+        out_specs=(hbm, hbm, hbm),
+        scratch_shapes=[dma((3,))],
+        name="write_results",
+    )(*results)
 
 
 def solution(mesh):

time: 89.1 us -> 100 us (1.12)
  Pallas kernels: 77.4 us -> 97.5 us
  local copies, waits for them, and re-layouts: 10.7 us -> 2.01 us
    pallas_call x1 -> x2, Pallas kernels: 77.4 us -> 97.5 us  [the longest x1 76.5 us: body(): pl.pallas_call(kernel, out_shape=tuple((pltpu.VMEM(shape, dtype) for shap...]
    unnamed x17 -> x6, local copies, waits for them, and re-layouts: 10.7 us -> 2.01 us
where the time goes in v2:
time: 100 us
  Pallas kernels  97.5 us (98%)
  local copies, waits for them, and re-layouts  2.01 us (2%)
    pallas_call x1, Pallas kernels, body(): pl.pallas_call(kernel, out_shape=tuple((pltpu.VMEM(shape, dtype) for shap...  76.5 us
    pallas_call x1, Pallas kernels, body(): pl.pallas_call(flush, out_shape=tuple((jax.ShapeDtypeStruct(shape, dtype)...  21 us
    unnamed x6, local copies, waits for them, and re-layouts  2.01 us

profile of v2, /device:TPU:1, one launch (start us, length us, event | category | flops | bytes accessed | tf_op | source)
XLA Modules:
  0.0 100.2 jit_solution(12214159430135317400)
XLA Ops:
  0.6 76.5 %expert_backward.1 = (bf16[1,128,512]{2,1,0:T(8,128)(2,1)S(1)}, f32[1,256,256]{2,1,0:T(8,128)S(1)}, f32[1,256,256]{2,1,0:T(8,128)S(1)}) custom-call(s32[1,128]{1,0:T(1,128)} %ids_hbm.1, s32[1,128]{1,0:T(1,128)} %slots_hbm.1, bf16[1,128,4096]{2,1,0:T(8,128)(2,1)} %tok_hbm.1, bf16[152,4096]{1,0:T(8,128)(2,1)} %bitcast.3, bf16[1,4096,256]{2,1,0:T(8,128)(2,1)} %wg_hbm.1, ...), custom_call_target="tpu_custom_call" | custom-call | tf_op jit(solution)/shard_map/expert_backward/pallas_call | solution.py:362
  77.2 0.0 copy-start
  77.2 0.7 copy-done
  77.9 0.0 copy-start.1
  77.9 0.7 copy-done.1
  78.5 0.0 copy-start.2
  78.6 0.6 copy-done.2
  79.2 21.0 %write_results.1 = (bf16[1,128,512]{2,1,0:T(8,128)(2,1)}, f32[1,256,256]{2,1,0:T(8,128)}, f32[1,256,256]{2,1,0:T(8,128)}) custom-call(bf16[1,128,512]{2,1,0:T(8,128)(2,1)} %copy-done.2, f32[1,256,256]{2,1,0:T(8,128)} %copy-done, f32[1,256,256]{2,1,0:T(8,128)} %copy-done.1), custom_call_target="tpu_custom_call" | custom-call | tf_op jit(solution)/shard_map/write_results/pallas_call | solution.py:411
Async XLA Ops:
  77.2 0.7 copy-start
  77.9 0.7 copy-start.1
  78.5 0.6 copy-start.2

commit v3 on v2

--- a/solution.py
+++ b/solution.py
@@ -19,6 +19,8 @@
 H = FEAT // 2
 FB = 256
 PACK = FEAT + 128
+SETS = 2
+SHARED = (4,)
 
 
 def mm(a, b, ca, cb):
@@ -38,7 +40,7 @@
     gi_out, gg_out, gu_out,
     ids, slots, tok, x, wg, wu, wd, route_out, route_in, routed, xt, pa, part, from_left, from_right, back_out, back_in, w_out, w_in, acc,
     load_sem, tok_sem, xload_sem,
-    route_ss, route_rs, xt_ss, xt_rs, tp_ss, tp_rs, dp_ss, dp_rs, rs_ss, rs_rs, back_ss, back_rs, w_ss, w_rs,
+    route_ss, route_rs, xt_ss, xt_rs, share_ss, share_rs, tp_ss, tp_rs, dp_ss, dp_rs, rs_ss, rs_rs, back_ss, back_rs, w_ss, w_rs,
 ):
     e, t, d = lax.axis_index("ctx"), lax.axis_index("tp"), lax.axis_index("dp")
     y, a = d // 2, d % 2
@@ -52,6 +54,7 @@
     def dpy(s):
         return {"dp": ((y + s + RING) % RING) * 2 + a}
 
+    over = {"tp": (t + 2 - 4 * (t % 4 // 2) + RING) % RING}
     twin = {"dp": y * 2 + 1 - a}
     started = []
 
@@ -68,8 +71,8 @@
     load_ids.start()
     load_slots.start()
     load_tok = []
-    for r, c, first in ((0, 0, t * 2), (0, 1, t * 2 + 1), (1, 0, (t + 4) % RING * 2), (1, 1, (t + 4) % RING * 2 + 1),
-                        (2, 0, (t + 5) % RING * 2 + 1), (2, 1, (t + 3) % RING * 2)):
+    for r, c in ((0, 0), (0, 1), (1, 0), (1, 1))[:2 * SETS]:
+        first = (t + 4 * r) % RING * 2 + c
         load_tok.append(
             pltpu.make_async_copy(
                 tok_hbm.at[0, :, pl.ds(pl.multiple_of(first * H, H), H)], tok.at[r, c], tok_sem.at[r, c]
@@ -89,7 +92,7 @@
     load_wd.start()
 
     barrier = pltpu.get_barrier_semaphore()
-    peers = [ctx(s) for s in range(1, RING)] + [tp(1), tp(-1)] + [dpy(s) for s in range(1, RING)] + [twin]
+    peers = [ctx(s) for s in range(1, RING)] + [tp(1), tp(-1)] + [dpy(s) for s in range(1, RING)] + [over, twin]
     for peer in peers:
         pl.semaphore_signal(barrier, inc=1, device_id=peer, device_id_type=MESH)
 
@@ -145,16 +148,41 @@
 
     for copy in load_x:
         copy.wait()
-    xts = {}
+    quarter = t % 4
+    lanes = pl.ds(pl.multiple_of(quarter % 2 * 128, 128), 128)
+    quarters, xts, shares = {}, {}, {}
+    for s in SHARED:
+        quarters[s] = send(
+            x.at[((y + s) % RING) * 2 + quarter // 2, :, lanes], xt.at[s, quarter // 2, :, lanes],
+            xt_ss.at[s, 0], xt_rs.at[s, 0], dpy(s),
+        )
     for s in (1, 7, 2, 6, 3, 5, 4):
         for h in range(2):
-            xts[s, h] = send(
-                x.at[((y + s) % RING) * 2 + h], xt.at[s, h], xt_ss.at[s, h], xt_rs.at[s, h], dpy(s)
-            )
+            if s not in SHARED:
+                xts[s, h] = send(
+                    x.at[((y + s) % RING) * 2 + h], xt.at[s, h], xt_ss.at[s, h], xt_rs.at[s, h], dpy(s)
+                )
     for h in range(2):
         xt[0, h] = x[y * 2 + h]
 
-    for r in (1, 2):
+    def share():
+        for s in SHARED:
+            quarters[s].wait_recv()
+            piece = xt.at[s, quarter // 2, :, lanes]
+            shares[s] = [
+                send(piece, piece, share_ss.at[s, n], share_rs.at[s, n], peer)
+                for n, peer in enumerate((tp(1), tp(-1), over))
+            ]
+
+    def saved_arrived(s):
+        if s in SHARED:
+            for copy in shares[s]:
+                copy.wait_recv()
+        elif s:
+            for h in range(2):
+                xts[s, h].wait_recv()
+
+    for r in range(1, SETS):
         pack(r)
         route.append(route_set(r))
 
@@ -172,15 +200,15 @@
                 flight[sign, 1, h] = ring_send(buf, ss, rs, 1, h, peer, sign)
         return flight
 
-    def ring_step(flight, buf, ss, rs, peer, k, h, last):
+    def ring_step(flight, buf, ss, rs, peer, k, h, part_):
         for sign in (1, -1):
             flight[sign, k, h].wait_recv()
-            if k < last - 1 or h == (0 if sign > 0 else 1):
+            if k < 3 or (part_ and h == (0 if sign > 0 else 1)):
                 flight[sign, k + 1, h] = ring_send(buf, ss, rs, k + 1, h, peer, sign)
 
-    def ring_end(flight, last):
-        flight[1, last, 0].wait_recv()
-        flight[-1, last, 1].wait_recv()
+    def ring_end(flight):
+        flight[1, 4, 0].wait_recv()
+        flight[-1, 4, 1].wait_recv()
 
     flight = ring_begin(routed, tp_ss, tp_rs, tp)
 
@@ -202,22 +230,23 @@
         return mm(routed[s, h], wd[:, pl.ds(pl.multiple_of(first, H), H)], 1, 1)
 
     grad_hidden = hidden_term(0, 0) + hidden_term(0, 1)
-    for k in range(1, 3):
+    for k in range(1, 4):
         for h in range(2):
-            ring_step(flight, routed, tp_ss, tp_rs, tp, k, h, 3)
+            ring_step(flight, routed, tp_ss, tp_rs, tp, k, h, SETS == 1)
             grad_hidden = grad_hidden + hidden_term(k, h) + hidden_term(RING - k, h)
-    unpack(1, ((4, 0), (4, 1)))
-    unpack(2, ((3, 1), (5, 0)))
-    for s, h in ((4, 0), (4, 1), (3, 1), (5, 0)):
-        grad_hidden = grad_hidden + hidden_term(s, h)
-    ring_end(flight, 3)
-    grad_hidden = grad_hidden + hidden_term(3, 0) + hidden_term(5, 1)
+        if k == 2 and SETS > 1:
+            unpack(1, ((4, 0), (4, 1)))
+            grad_hidden = grad_hidden + hidden_term(4, 0) + hidden_term(4, 1)
+    if SETS == 1:
+        ring_end(flight)
+        grad_hidden = grad_hidden + hidden_term(4, 0) + hidden_term(4, 1)
 
     grad_gate_pre = (grad_hidden * gate_factor).astype(BF16)
     grad_up_pre = (grad_hidden * up_factor).astype(BF16)
     pa[0, 0] = grad_gate_pre
     pa[0, 1] = grad_up_pre
     dp_flight = ring_begin(pa, dp_ss, dp_rs, dpy)
+    share()
 
     def partial_term(j, h):
         first = pl.ds(pl.multiple_of(((t + j) % RING) * FEAT + h * H, H), H)
@@ -252,12 +281,10 @@
     partial_term(5, 1)
 
     def dp_step(k, h):
-        ring_step(dp_flight, pa, dp_ss, dp_rs, dpy, k, h, 4)
+        ring_step(dp_flight, pa, dp_ss, dp_rs, dpy, k, h, True)
 
     def weight_term(s):
-        if s:
-            for h in range(2):
-                xts[s, h].wait_recv()
+        saved_arrived(s)
         for half in range(2):
             for which in range(2):
                 term = mm(xt[s, half], pa[s, which], 0, 0)
@@ -292,9 +319,8 @@
     dp_step(3, 1)
     weight_term(3)
     weight_term(5)
-    for h in range(2):
-        xts[4, h].wait_recv()
-    ring_end(dp_flight, 4)
+    saved_arrived(4)
+    ring_end(dp_flight)
     w_flight = []
     for which in range(2):
         w_out[which] = (acc[1 - a, which] + mm(xt[4, 1 - a], pa[4, which], 0, 0)).astype(BF16)
@@ -337,17 +363,6 @@
         copy.wait_send()
 
 
-def flush(gi, gg, gu, gi_out, gg_out, gu_out, sems):
-    copies = [
-        pltpu.make_async_copy(src, dst, sems.at[n])
-        for n, (src, dst) in enumerate(((gi, gi_out), (gg, gg_out), (gu, gu_out)))
-    ]
-    for copy in copies:
-        copy.start()
-    for copy in copies:
-        copy.wait()
-
-
 def body(grad_out, expert_input, expert_ids, slots, w_gate, w_up, w_down):
     saved = expert_input.transpose(0, 1, 3, 2, 4).reshape(ROWS, D)
     vmem = pl.BlockSpec(memory_space=pltpu.VMEM)
@@ -359,7 +374,7 @@
         pltpu.with_memory_space_constraint(operand, pltpu.HBM)
         for operand in (expert_ids, slots, grad_out, saved, w_gate, w_up, w_down)
     ]
-    results = pl.pallas_call(
+    return pl.pallas_call(
         kernel,
         out_shape=tuple(pltpu.VMEM(shape, dtype) for shape, dtype in shapes),
         in_specs=[hbm] * 7,
@@ -367,13 +382,13 @@
         scratch_shapes=[
             pltpu.VMEM((1, TOK), jnp.int32),
             pltpu.VMEM((1, TOK), jnp.int32),
-            pltpu.VMEM((3, 2, TOK, H), BF16),
+            pltpu.VMEM((SETS, 2, TOK, H), BF16),
             pltpu.VMEM((2 * RING, ROWS, H), BF16),
             pltpu.VMEM((D, FB), BF16),
             pltpu.VMEM((D, FB), BF16),
             pltpu.VMEM((FB, D), BF16),
-            pltpu.VMEM((3, RING, MAIN, PACK), BF16),
-            pltpu.VMEM((3, RING, MAIN, PACK), BF16),
+            pltpu.VMEM((SETS, RING, MAIN, PACK), BF16),
+            pltpu.VMEM((SETS, RING, MAIN, PACK), BF16),
             pltpu.VMEM((RING,) + piece, BF16),
             pltpu.VMEM((RING,) + piece, BF16),
             pltpu.VMEM((RING,) + piece, BF16),
@@ -386,12 +401,14 @@
             pltpu.VMEM((2, 256, FB), BF16),
             pltpu.VMEM((2, 2, 256, FB), F32),
             dma((6,)),
-            dma((3, 2)),
+            dma((SETS, 2)),
             dma((2 * RING,)),
-            dma((3, RING)),
-            dma((3, RING)),
+            dma((SETS, RING)),
+            dma((SETS, RING)),
             dma((RING, 2)),
             dma((RING, 2)),
+            dma((RING, 3)),
+            dma((RING, 3)),
             dma((2, 4, 2)),
             dma((2, 4, 2)),
             dma((2, 4, 2)),
@@ -408,14 +425,6 @@
         ),
         name="expert_backward",
     )(*operands)
-    return pl.pallas_call(
-        flush,
-        out_shape=tuple(jax.ShapeDtypeStruct(shape, dtype) for shape, dtype in shapes),
-        in_specs=[hbm] * 3,
-        out_specs=(hbm, hbm, hbm),
-        scratch_shapes=[dma((3,))],
-        name="write_results",
-    )(*results)
 
 
 def solution(mesh):

time: 100 us -> 76.4 us (0.76)
  Pallas kernels: 97.5 us -> 73.5 us
    pallas_call x1 -> x0, Pallas kernels: 21 us -> none  [body(): pl.pallas_call(flush, out_shape=tuple((jax.ShapeDtypeStruct(shape, dtype)...]
    pallas_call x1, Pallas kernels: 76.5 us -> 73.5 us  [body(): pl.pallas_call(kernel, out_shape=tuple((pltpu.VMEM(shape, dtype) for shap...]
    unnamed x6 -> x3, local copies, waits for them, and re-layouts: 2.01 us -> 2.06 us
where the time goes in v3:
time: 76.4 us; the launch traced here: 76.2 us
  Pallas kernels  73.5 us (96%)
  local copies, waits for them, and re-layouts  2.06 us (3%)
    pallas_call x1, Pallas kernels, body(): pl.pallas_call(kernel, out_shape=tuple((pltpu.VMEM(shape, dtype) for shap...  73.5 us
    unnamed x3, local copies, waits for them, and re-layouts  2.06 us

profile of v3, /device:TPU:1, one launch (start us, length us, event | category | flops | bytes accessed | tf_op | source)
XLA Modules:
  0.0 76.2 jit_solution(14458630603956649936)
XLA Ops:
  0.6 73.5 %expert_backward.1 = (bf16[1,128,512]{2,1,0:T(8,128)(2,1)S(1)}, f32[1,256,256]{2,1,0:T(8,128)S(1)}, f32[1,256,256]{2,1,0:T(8,128)S(1)}) custom-call(s32[1,128]{1,0:T(1,128)} %ids_hbm.1, s32[1,128]{1,0:T(1,128)} %slots_hbm.1, bf16[1,128,4096]{2,1,0:T(8,128)(2,1)} %tok_hbm.1, bf16[152,4096]{1,0:T(8,128)(2,1)} %bitcast.3, bf16[1,4096,256]{2,1,0:T(8,128)(2,1)} %wg_hbm.1, ...), custom_call_target="tpu_custom_call" | custom-call | tf_op jit(solution)/shard_map/expert_backward/pallas_call | solution.py:377
  74.2 0.7 copy.13
  74.8 0.7 copy.14
  75.5 0.7 copy.15

commit v4 on v3

--- a/solution.py
+++ b/solution.py
@@ -79,6 +79,11 @@
             )
         )
         load_tok[-1].start()
+    barrier = pltpu.get_barrier_semaphore()
+    peers = [ctx(s) for s in range(1, RING)] + [tp(1), tp(-1)] + [dpy(s) for s in range(1, RING)] + [over, twin]
+    for peer in peers:
+        pl.semaphore_signal(barrier, inc=1, device_id=peer, device_id_type=MESH)
+
     load_x = [
         pltpu.make_async_copy(x_hbm.at[:, pl.ds(j * H, H)], x.at[j], xload_sem.at[j]) for j in range(2 * RING)
     ]
@@ -91,25 +96,20 @@
     load_wu.start()
     load_wd.start()
 
-    barrier = pltpu.get_barrier_semaphore()
-    peers = [ctx(s) for s in range(1, RING)] + [tp(1), tp(-1)] + [dpy(s) for s in range(1, RING)] + [over, twin]
-    for peer in peers:
-        pl.semaphore_signal(barrier, inc=1, device_id=peer, device_id_type=MESH)
+    rows = iota((TOK, TOK), 0)
+    cols = iota((TOK, TOK), 1)
+    main_map = onehot(cols == (rows % RING) * MAIN + rows // RING)
+    erow = iota((3 * RING, TOK), 0)
+    ecol = iota((3 * RING, TOK), 1)
+    fold_map = [onehot(ecol == (erow % RING) * MAIN + 4 * (erow // RING) + q) for q in range(4)]
 
     load_ids.wait()
     load_slots.wait()
     expert, slot = ids[...], slots[...]
     main_row = jnp.where(slot < MAIN, expert * MAIN + slot, -1)
     fold_row = jnp.where(slot < MAIN, -8, expert * MAIN + 4 * (slot - MAIN))
-    rows = iota((TOK, TOK), 0)
     to_main = onehot(rows == main_row)
     to_fold = [onehot(rows == fold_row + q) for q in range(4)]
-    cols = iota((TOK, TOK), 1)
-    main_map = onehot(cols == (rows % RING) * MAIN + rows // RING)
-    erow = iota((3 * RING, TOK), 0)
-    ecol = iota((3 * RING, TOK), 1)
-    fold_map = [onehot(ecol == (erow % RING) * MAIN + 4 * (erow // RING) + q) for q in range(4)]
-
     def pack(r):
         load_tok[2 * r].wait()
         load_tok[2 * r + 1].wait()
@@ -142,7 +142,8 @@
             routed[s, h, TOK:, :128] = fold_part[2 * c]
             routed[s, h, TOK:, 128:] = fold_part[2 * c + 1]
 
-    pack(0)
+    for r in range(SETS):
+        pack(r)
     pl.semaphore_wait(barrier, len(peers))
     route = [route_set(0)]
 
@@ -182,10 +183,6 @@
             for h in range(2):
                 xts[s, h].wait_recv()
 
-    for r in range(1, SETS):
-        pack(r)
-        route.append(route_set(r))
-
     unpack(0, ((0, 0), (0, 1)))
 
     def ring_send(buf, ss, rs, k, h, peer, sign):
@@ -211,6 +208,8 @@
         flight[-1, 4, 1].wait_recv()
 
     flight = ring_begin(routed, tp_ss, tp_rs, tp)
+    for r in range(1, SETS):
+        route.append(route_set(r))
 
     load_wg.wait()
     load_wu.wait()
@@ -246,7 +245,6 @@
     pa[0, 0] = grad_gate_pre
     pa[0, 1] = grad_up_pre
     dp_flight = ring_begin(pa, dp_ss, dp_rs, dpy)
-    share()
 
     def partial_term(j, h):
         first = pl.ds(pl.multiple_of(((t + j) % RING) * FEAT + h * H, H), H)
@@ -277,6 +275,7 @@
     sum_send(1, 3, 1)
     partial_term(5, 0)
     sum_send(-1, 3, 0)
+    share()
     partial_term(3, 0)
     partial_term(5, 1)
 
@@ -319,31 +318,59 @@
     dp_step(3, 1)
     weight_term(3)
     weight_term(5)
-    saved_arrived(4)
-    ring_end(dp_flight)
-    w_flight = []
-    for which in range(2):
-        w_out[which] = (acc[1 - a, which] + mm(xt[4, 1 - a], pa[4, which], 0, 0)).astype(BF16)
-        w_flight.append(send(w_out.at[which], w_in.at[which], w_ss.at[which], w_rs.at[which], twin))
-
-    for h in (1, 0):
-        rs_flight[1, 1, h].wait_recv()
-        rs_flight[-1, 1, h].wait_recv()
-    slot_grad = [
-        (part[0, h].astype(F32) + from_left[0, h].astype(F32) + from_right[0, h].astype(F32)).astype(BF16)
-        for h in range(2)
+    def prepared(src, dst, ss, rs, dev):
+        return pltpu.make_async_remote_copy(
+            src_ref=src, dst_ref=dst, send_sem=ss, recv_sem=rs, device_id=dev, device_id_type=MESH
+        )
+
+    sent = len(started)
+    w_flight = [
+        prepared(w_out.at[which], w_in.at[which], w_ss.at[which], w_rs.at[which], twin) for which in range(2)
     ]
-    for h in range(2):
-        back_out[:, :, h * H:h * H + H] = mm(main_map, slot_grad[h][:TOK, :], 0, 0).astype(BF16).reshape(RING, MAIN, H)
-    folded = mm(fold_map[0], slot_grad[0][TOK:, :128], 0, 0)
-    for q in range(1, 4):
-        folded = folded + mm(fold_map[q], slot_grad[q // 2][TOK:, (q % 2) * 128:(q % 2) * 128 + 128], 0, 0)
-    back_out[:, :, FEAT:] = folded.astype(BF16).reshape(RING, MAIN, 128)
-    back_in[e] = back_out[e]
     back = [
-        send(back_out.at[(e + s) % RING], back_in.at[e], back_ss.at[s], back_rs.at[s], ctx(s)) for s in range(1, RING)
+        prepared(back_out.at[(e + s) % RING], back_in.at[e], back_ss.at[s], back_rs.at[s], ctx(s))
+        for s in range(1, RING)
     ]
-
+    started.extend(w_flight + back)
+
+    def send_weights():
+        saved_arrived(4)
+        ring_end(dp_flight)
+        for which in range(2):
+            w_out[which] = (acc[1 - a, which] + mm(xt[4, 1 - a], pa[4, which], 0, 0)).astype(BF16)
+            w_flight[which].start()
+
+    def send_back():
+        for h in (1, 0):
+            rs_flight[1, 1, h].wait_recv()
+            rs_flight[-1, 1, h].wait_recv()
+        slot_grad = [
+            (part[0, h].astype(F32) + from_left[0, h].astype(F32) + from_right[0, h].astype(F32)).astype(BF16)
+            for h in range(2)
+        ]
+        for h in range(2):
+            main_rows = mm(main_map, slot_grad[h][:TOK, :], 0, 0).astype(BF16)
+            back_out[:, :, h * H:h * H + H] = main_rows.reshape(RING, MAIN, H)
+        folded = mm(fold_map[0], slot_grad[0][TOK:, :128], 0, 0)
+        for q in range(1, 4):
+            folded = folded + mm(fold_map[q], slot_grad[q // 2][TOK:, (q % 2) * 128:(q % 2) * 128 + 128], 0, 0)
+        back_out[:, :, FEAT:] = folded.astype(BF16).reshape(RING, MAIN, 128)
+        for copy in back:
+            copy.start()
+        back_in[e] = back_out[e]
+
+    @pl.when(a == 1)
+    def weights_first():
+        send_weights()
+        send_back()
+
+    @pl.when(a == 0)
+    def back_first():
+        send_back()
+        send_weights()
+
+    for copy in started[:sent]:
+        copy.wait_send()
     own = [acc[a, which] + mm(xt[4, a], pa[4, which], 0, 0) for which in range(2)]
 
     for copy in back:
@@ -359,7 +386,7 @@
         w_flight[which].wait_recv()
         out[0] = (own[which] + w_in[which].astype(F32)) * (1.0 / 16.0)
 
-    for copy in started:
+    for copy in started[sent:]:
         copy.wait_send()
 
 

time: 76.4 us -> 72.9 us (0.954); the launches traced: 76.2 us -> 71.5 us
  Pallas kernels: 73.5 us -> 68.8 us
    pallas_call x1, Pallas kernels: 73.5 us -> 68.8 us  [body(): pl.pallas_call(kernel, out_shape=tuple((pltpu.VMEM(shape, dtype) for shap...]
where the time goes in v4:
time: 72.9 us; the launch traced here: 71.5 us
  Pallas kernels  68.8 us (94%)
  local copies, waits for them, and re-layouts  2.06 us (3%)
    pallas_call x1, Pallas kernels, body(): pl.pallas_call(kernel, out_shape=tuple((pltpu.VMEM(shape, dtype) for shap...  68.8 us
    unnamed x3, local copies, waits for them, and re-layouts  2.06 us

profile of v4, /device:TPU:1, one launch (start us, length us, event | category | flops | bytes accessed | tf_op | source)
XLA Modules:
  0.0 71.5 jit_solution(13859163447103047554)
XLA Ops:
  0.6 68.8 %expert_backward.1 = (bf16[1,128,512]{2,1,0:T(8,128)(2,1)S(1)}, f32[1,256,256]{2,1,0:T(8,128)S(1)}, f32[1,256,256]{2,1,0:T(8,128)S(1)}) custom-call(s32[1,128]{1,0:T(1,128)} %ids_hbm.1, s32[1,128]{1,0:T(1,128)} %slots_hbm.1, bf16[1,128,4096]{2,1,0:T(8,128)(2,1)} %tok_hbm.1, bf16[152,4096]{1,0:T(8,128)(2,1)} %bitcast.3, bf16[1,4096,256]{2,1,0:T(8,128)(2,1)} %wg_hbm.1, ...), custom_call_target="tpu_custom_call" | custom-call | tf_op jit(solution)/shard_map/expert_backward/pallas_call | solution.py:404
  69.4 0.7 copy.13
  70.1 0.7 copy.14
  70.8 0.7 copy.15

commit v5 on v4

--- a/solution.py
+++ b/solution.py
@@ -234,6 +234,7 @@
             ring_step(flight, routed, tp_ss, tp_rs, tp, k, h, SETS == 1)
             grad_hidden = grad_hidden + hidden_term(k, h) + hidden_term(RING - k, h)
         if k == 2 and SETS > 1:
+            share()
             unpack(1, ((4, 0), (4, 1)))
             grad_hidden = grad_hidden + hidden_term(4, 0) + hidden_term(4, 1)
     if SETS == 1:
@@ -244,7 +245,6 @@
     grad_up_pre = (grad_hidden * up_factor).astype(BF16)
     pa[0, 0] = grad_gate_pre
     pa[0, 1] = grad_up_pre
-    dp_flight = ring_begin(pa, dp_ss, dp_rs, dpy)
 
     def partial_term(j, h):
         first = pl.ds(pl.multiple_of(((t + j) % RING) * FEAT + h * H, H), H)
@@ -271,11 +271,11 @@
     sum_send(1, 4, 0)
     partial_term(4, 1)
     sum_send(-1, 4, 1)
+    dp_flight = ring_begin(pa, dp_ss, dp_rs, dpy)
     partial_term(3, 1)
     sum_send(1, 3, 1)
     partial_term(5, 0)
     sum_send(-1, 3, 0)
-    share()
     partial_term(3, 0)
     partial_term(5, 1)
 
@@ -289,30 +289,30 @@
                 term = mm(xt[s, half], pa[s, which], 0, 0)
                 acc[half, which] = acc[half, which] + term if s else term
 
-    dp_step(1, 0)
     sum_step(1, 3, 0)
     sum_step(-1, 3, 1)
+    dp_step(1, 0)
     for j in (2, 6):
         for h in range(2):
             partial_term(j, h)
-    dp_step(1, 1)
     sum_step(1, 2, 1)
     sum_step(-1, 2, 0)
+    dp_step(1, 1)
     weight_term(0)
-    dp_step(2, 0)
     sum_step(1, 2, 0)
     sum_step(-1, 2, 1)
+    dp_step(2, 0)
     for j in (1, 7, 0):
         for h in range(2):
             partial_term(j, h)
-    dp_step(2, 1)
     sum_step(1, 1, 1)
     sum_step(-1, 1, 0)
+    dp_step(2, 1)
     weight_term(1)
     weight_term(7)
-    dp_step(3, 0)
     sum_step(1, 1, 0)
     sum_step(-1, 1, 1)
+    dp_step(3, 0)
     weight_term(2)
     weight_term(6)
     dp_step(3, 1)
@@ -359,12 +359,12 @@
             copy.start()
         back_in[e] = back_out[e]
 
-    @pl.when(a == 1)
+    @pl.when(e < 2)
     def weights_first():
         send_weights()
         send_back()
 
-    @pl.when(a == 0)
+    @pl.when(e >= 2)
     def back_first():
         send_back()
         send_weights()

time: 72.9 us -> 72.4 us (level)
  the two profiles are of different devices: /device:TPU:1 before, /device:TPU:10 now
where the time goes in v5:
time: 72.4 us; the launch traced here: 72.3 us
  Pallas kernels  69.6 us (96%)
  local copies, waits for them, and re-layouts  2.06 us (3%)
    pallas_call x1, Pallas kernels, body(): pl.pallas_call(kernel, out_shape=tuple((pltpu.VMEM(shape, dtype) for shap...  69.6 us
    unnamed x3, local copies, waits for them, and re-layouts  2.06 us

profile of v5, /device:TPU:10, one launch (start us, length us, event | category | flops | bytes accessed | tf_op | source)
XLA Modules:
  0.0 72.3 jit_solution(1531162274456630300)
XLA Ops:
  0.6 69.6 %expert_backward.1 = (bf16[1,128,512]{2,1,0:T(8,128)(2,1)S(1)}, f32[1,256,256]{2,1,0:T(8,128)S(1)}, f32[1,256,256]{2,1,0:T(8,128)S(1)}) custom-call(s32[1,128]{1,0:T(1,128)} %ids_hbm.1, s32[1,128]{1,0:T(1,128)} %slots_hbm.1, bf16[1,128,4096]{2,1,0:T(8,128)(2,1)} %tok_hbm.1, bf16[152,4096]{1,0:T(8,128)(2,1)} %bitcast.3, bf16[1,4096,256]{2,1,0:T(8,128)(2,1)} %wg_hbm.1, ...), custom_call_target="tpu_custom_call" | custom-call | tf_op jit(solution)/shard_map/expert_backward/pallas_call | solution.py:404
  70.2 0.7 copy.13
  70.9 0.7 copy.14
  71.6 0.7 copy.15
